TPU v7x, 128 devices: a whole 4x4x4 slice. The times are simulated.
128 devices in a mesh: surf: 4 (over z_hi, core), shot: 32 (over z_lo, x, y).
Axes of the slice: x: 4, y: 4, z: 4 (z_hi: 2, z_lo: 2; z = z_hi * 2 + z_lo), core: 2. Of those that a mesh axis runs over, the one named last changes fastest.
Arguments:
- traces: bfloat16 [256, 640, 1024], P('shot'), may hold values from -6 to 6
- surface_point: int32 [4, 4, 2], replicated, may hold values from 0 to 639, as said below
- gather_index: int32 [4, 4, 2], replicated, may hold values from 0 to 255, as said below
Outputs:
- prediction: bfloat16 [256, 640, 1024], P('shot', 'surf')
Inputs may be any that keep to these rules, and one draw needn't show every extreme that they name: `surface_point`: all 32 entries are distinct. `gather_index`: the 2 entries of one round and group are distinct and lie on one index of shot: they share their quotient by 8.
All inputs are finite; a program needn't handle non-finite values.
Results may differ from a plain program's by a relative error of at most 0.015.
Values may be sent and summed in bfloat16 or wider, within the bound.
A program may use at most 128 MiB of HBM per device.

v0:
```python
import functools
import math

import jax
import jax.numpy as jnp
import ml_dtypes
import numpy as np
from jax import lax
from jax.experimental import pallas as pl
from jax.experimental.pallas import tpu as pltpu
from jax.sharding import PartitionSpec as P

F = 256
OWNERS = 32
BINS = F // OWNERS
PART = 2 * BINS
SHOTS = 8
POINTS = 32
MAIN, TAIL = 128, 32
SHARE = MAIN + TAIL
HALF = POINTS // 2
WIDE = SHOTS * TAIL
MESH = pl.DeviceIdType.MESH
ROOMS = (4, 6, 8)
F32, BF16 = jnp.float32, jnp.bfloat16


def dft_rows(samples):
    freq = np.arange(F).reshape(OWNERS // 2, BINS, 2).transpose(2, 0, 1).reshape(OWNERS, 1, BINS, 1)
    angles = (freq * np.arange(samples) % samples) * (2.0 * math.pi / samples)
    table = np.concatenate([np.cos(angles), -np.sin(angles)], axis=1)
    table = table.astype(np.float32).astype(ml_dtypes.bfloat16).astype(np.float32)
    scaled = table.reshape(2 * F, samples) * samples**-0.5
    return scaled.astype(ml_dtypes.bfloat16)


def offsets():
    steps = [(z, x, y) for z in range(2) for x in range(4) for y in range(4)][1:]
    return sorted(steps, key=lambda k: -(k[0] + min(k[1], 4 - k[1]) + min(k[2], 4 - k[2])))


def wide_rows(ref, rows):
    return jnp.concatenate([ref[half, rows, :] for half in range(2)], axis=1)


def dot(a, b, contract):
    return lax.dot_general(a, b, (contract, ((), ())), preferred_element_type=F32)


def iota(shape, axis):
    return lax.broadcasted_iota(jnp.int32, shape, axis)


def product(left, right):
    real, imag = right
    both = jnp.concatenate(
        [jnp.concatenate([real, imag], axis=1), jnp.concatenate([-imag, real], axis=1)], axis=0
    )
    return dot(left, both, ((1,), (0,)))


def kernel(
    slots,
    point_ref, gather_ref, traces, table, hm, ht,
    points, gathers, slot_v, slot_of, tab, block, full, xn, sm, sn, st, rm, rn, other, rt,
    near, lhs, far_main, far_tail, om, ot, bm, bt,
    load_sem, pair_sem, send_sem, recv_sem,
):
    group, me = lax.axis_index("surf"), lax.axis_index("shot")
    core = group % 2
    z, x, y = me // 16, (me // 4) % 4, me % 4
    peers = [(z ^ k) * 16 + (x + i) % 4 * 4 + (y + j) % 4 for k, i, j in offsets()]
    away = lambda d: [n for n, step in enumerate(offsets()) if sum(map(bool, step)) == d]
    everyone = sorted(range(len(peers)), key=lambda n: (n * 12) % 31)
    groups = lax.axis_size("surf")

    share = SHARE // PART
    blocks = [pl.ds((group + k) % groups * share, share) for k in range(groups)]
    loads = [
        pltpu.make_async_copy(table, tab, load_sem.at[0]),
        pltpu.make_async_copy(traces.at[:, blocks[0]], block, load_sem.at[1]),
    ]
    for k in range(1, groups):
        part = traces.at[:, blocks[k]], full.at[:, blocks[k]]
        loads.append(pltpu.make_async_copy(*part, load_sem.at[1 + k]))
    loads.append(pltpu.make_async_copy(point_ref, points, load_sem.at[5]))
    loads.append(pltpu.make_async_copy(gather_ref, gathers, load_sem.at[6]))
    for load in loads[:2] + loads[5:]:
        load.start()
    barrier = pltpu.get_barrier_semaphore()
    pl.semaphore_signal(barrier, inc=1, device_id=(group ^ 1, me), device_id_type=MESH)
    for n in everyone:
        pl.semaphore_signal(barrier, inc=1, device_id=(group, peers[n]), device_id_type=MESH)
    for load in loads[2:5]:
        load.start()

    def start(way):
        kind, source, target = way
        pltpu.make_async_copy(source(me), target(me), recv_sem.at[kind]).start()
        for n in everyone:
            pltpu.make_async_remote_copy(
                src_ref=source(peers[n]),
                dst_ref=target(me),
                send_sem=send_sem.at[kind],
                recv_sem=recv_sem.at[kind],
                device_id=(group, peers[n]),
                device_id_type=MESH,
            ).start()

    def arrive(kind, whole):
        pltpu.make_async_copy(whole, whole, recv_sem.at[kind]).wait()

    def sent(kind, whole):
        others = whole.at[pl.ds(0, OWNERS - 1)]
        pltpu.make_async_copy(others, others, send_sem.at[kind]).wait()

    def forward(rows):
        spectra = dot(tab[...], rows, ((1,), (1,))).astype(BF16)
        return spectra.reshape(OWNERS, PART, -1)

    slot = lambda ref: lambda device: ref.at[device]
    two = lambda ref, k: lambda device: ref.at[device, pl.ds(2 * k, 2)]
    rounds = range(slots // 2)
    early = 0 if slots == ROOMS[0] else 1
    pairs = range(SHOTS // 2)
    tail_way, near_way = (0, slot(st), slot(rt)), (1, slot(sn), slot(rn))
    main_ways = [(2, two(sm, k), two(rm, k)) for k in rounds]

    for load in loads[5:]:
        load.wait()
    index = lambda i: gathers[i // 8, i // 4 % 2, i % 4]
    owner = lambda i: lax.div(index(i), SHOTS)
    if slots < SHOTS:
        wanted = wanted_of(index)
        before = jnp.zeros((1, MAIN), jnp.int32)
        for l in range(SHOTS):
            row = wanted[l : l + 1]
            slot_v[l : l + 1] = before + SHOTS * row
            before = before + row
        table_copy = pltpu.make_async_copy(slot_v, slot_of, load_sem.at[7])
        table_copy.start()
        table_copy.wait()
        mine = [0] * SHOTS
        for l in range(SHOTS):
            for k in range(slots):
                mine[k] = jnp.where(slot_of[l, me] == SHOTS + k, l, mine[k])
        place = lambda i: slot_of[lax.rem(index(i), SHOTS), owner(i)] - SHOTS
    else:
        mine = range(SHOTS)
        place = lambda i: lax.rem(index(i), SHOTS)

    loads[0].wait()
    loads[1].wait()
    spread_own = pltpu.make_async_copy(block, full.at[:, blocks[0]], load_sem.at[8])
    spread_own.start()
    main, tail = pl.ds(0, MAIN // PART), pl.ds(MAIN // PART, TAIL // PART)
    tails = st.shape[2] // TAIL
    rows = [block[mine[k], tail].reshape(TAIL, -1) for k in range(tails)]
    st[...] = forward(jnp.concatenate(rows, axis=0))
    for k in rounds:
        rows = [block[mine[2 * k + j], main].reshape(MAIN, -1) for j in range(2)]
        spectra = forward(jnp.concatenate(rows, axis=0))
        sm[:, 2 * k] = spectra[..., :MAIN]
        sm[:, 2 * k + 1] = spectra[..., MAIN:]

    pl.semaphore_wait(barrier, len(everyone) + 1)
    for way in (tail_way, *main_ways[:early]):
        start(way)

    for load in (*loads[2:5], spread_own):
        load.wait()
    chosen = jnp.zeros((HALF, 1), jnp.int32)
    aligned = []
    for i in range(HALF):
        point = points[core * 2 + i // 8, i // 4 % 2, i % 4]
        aligned.append(lax.div(point, PART))
        chosen = jnp.where(iota((HALF, 1), 0) == i, i * PART + lax.rem(point, PART), chosen)
    pick = (iota((HALF, HALF * PART), 1) == chosen).astype(BF16)
    for s in range(SHOTS):
        rows = jnp.concatenate([full[s, row] for row in aligned], axis=0)
        xn[s * HALF : (s + 1) * HALF, :] = dot(pick, rows, ((1,), (0,))).astype(BF16)
    sn[...] = forward(xn[...])
    for way in (near_way, *main_ways[early:]):
        start(way)

    lines = [[pl.ds(part * BINS + b, OWNERS, stride=PART) for part in range(2)] for b in range(BINS)]
    slot_at = iota((PART, st.shape[2]), 1) // TAIL
    wide = (st.shape[2], WIDE)
    spread = (iota(wide, 0) % TAIL == iota(wide, 1) % TAIL).astype(BF16)
    shot_of_point = lambda axis: iota((WIDE, WIDE), axis) % MAIN // HALF
    tile = lambda a: jnp.concatenate([a[:HALF]] * SHOTS + [a[HALF:]] * SHOTS, axis=0)

    arrive(0, rt)
    picked = []
    for i in range(POINTS):
        picked.append(rt[owner(i)] * (slot_at == place(i)).astype(BF16))
    spectra = dot(jnp.concatenate(picked, axis=0), spread, ((1,), (0,)))
    for half in range(2):
        far_tail[half] = spectra[:, half * MAIN : (half + 1) * MAIN]
    arrive(1, rn)
    swap = pltpu.make_async_remote_copy(
        src_ref=rn,
        dst_ref=other,
        send_sem=pair_sem.at[0],
        recv_sem=pair_sem.at[1],
        device_id=(group ^ 1, me),
        device_id_type=MESH,
    )
    swap.start()
    near[core] = rn[...].reshape(OWNERS * PART, MAIN).astype(F32)
    swap.wait()
    near[1 - core] = other[...].reshape(OWNERS * PART, MAIN).astype(F32)
    diagonal = (shot_of_point(0) == iota((WIDE, WIDE), 1) // TAIL).astype(BF16)
    for b in range(BINS):
        left = jnp.concatenate([wide_rows(near, r).astype(BF16) for r in lines[b]], axis=1)
        right = [tile(wide_rows(far_tail, r).astype(BF16)) * diagonal for r in lines[b]]
        total = -product(left, right)
        for part in range(2):
            for half in range(2):
                lanes = slice(part * WIDE + half * MAIN, part * WIDE + (half + 1) * MAIN)
                ot[half, lines[b][part], :] = total[:, lanes]
    for half in range(2):
        lanes = slice(half * MAIN, (half + 1) * MAIN)
        bt[:, :, lanes] = ot[half].reshape(OWNERS, PART, MAIN).astype(BF16)
    back_tail = 3, slot(bt), slot(ht)
    start(back_tail)
    diagonal = (iota((WIDE, WIDE), 0) // OWNERS == shot_of_point(1)).astype(BF16)
    for b in range(BINS):
        for part, r in enumerate(lines[b]):
            copies = [wide_rows(near, r).astype(BF16)] * SHOTS
            lhs[b, :, part * WIDE : (part + 1) * WIDE] = jnp.concatenate(copies, axis=0) * diagonal

    arrive(2, rm)
    for i in range(POINTS):
        far_main[i * PART : (i + 1) * PART, :] = rm[owner(i), place(i)].astype(F32)
    for b in range(BINS):
        total = -product(lhs[b], [tile(far_main[r, :].astype(BF16)) for r in lines[b]])
        for s in range(SHOTS):
            for part in range(2):
                om[pl.ds(s * PART + part * BINS + b, OWNERS, stride=SHOTS * PART), :] = total[
                    s * OWNERS : (s + 1) * OWNERS, part * MAIN : (part + 1) * MAIN
                ]
    totals = om[...].reshape(OWNERS, SHOTS, PART, MAIN)
    four = lambda ref, k: lambda device: ref.at[device, pl.ds(4 * k, 4)]
    for k in range(2):
        bm[:, 4 * k : 4 * k + 4] = totals[:, 4 * k : 4 * k + 4].astype(BF16)
        back_main = 4, four(bm, k), four(hm, k)
        start(back_main)
    arrive(3, ht)
    arrive(4, hm)
    for kind, whole in enumerate((st, sn, sm, bt, bm)):
        sent(kind, whole)


def wanted_of(index):
    gather = iota((SHOTS, MAIN), 1) * SHOTS + iota((SHOTS, MAIN), 0)
    wanted = jnp.zeros((SHOTS, MAIN), jnp.int32)
    for i in range(POINTS):
        wanted = jnp.where(gather == index(i), 1, wanted)
    return wanted


def choose(gathers, case):
    wanted = wanted_of(lambda i: gathers[i // 8, i // 4 % 2, i % 4])
    most = jnp.max(jnp.sum(wanted, axis=0, keepdims=True))
    case[0] = sum((most > room).astype(jnp.int32) for room in ROOMS[:-1])


def inverse(hm, ht, tab, out, series, store_sem):
    shots, _, samples = out.shape
    pairs = range(shots // 2)
    def invert(spectra, two, receivers):
        even = dot(spectra[:F], tab[:F], ((0,), (0,)))
        odd = dot(spectra[F:], tab[F:], ((0,), (0,)))
        shape = (two.stop - two.start, receivers.stop - receivers.start, samples // 2)
        series[two, receivers, : samples // 2] = (even + odd).astype(BF16).reshape(shape)
        series[two, receivers, samples // 2 :] = (even - odd).astype(BF16).reshape(shape)

    invert(ht[...].reshape(2 * F, WIDE), slice(0, shots), slice(MAIN, SHARE))
    stores = []
    for k in pairs:
        two = pl.ds(2 * k, 2)
        spectra = [hm[:, 2 * k + s].reshape(2 * F, MAIN) for s in range(2)]
        invert(jnp.concatenate(spectra, axis=1), slice(2 * k, 2 * k + 2), slice(0, MAIN))
        stores.append(pltpu.make_async_copy(series.at[two], out.at[two], store_sem.at[k]))
        stores[-1].start()
    for store in stores:
        store.wait()


def tail_lanes(slots):
    return MAIN if slots * TAIL <= MAIN else WIDE


def shards(traces, surface_point, gather_index):
    shots, receivers, samples = traces.shape
    vmem = lambda *shape, dtype=BF16: pltpu.VMEM(shape, dtype)
    hbm, anywhere = pl.BlockSpec(memory_space=pltpu.HBM), pl.BlockSpec(memory_space=pl.ANY)
    message = lambda lanes: vmem(OWNERS, PART, lanes)
    table = dft_rows(samples)
    back = [
        jax.ShapeDtypeStruct((OWNERS, SHOTS, PART, MAIN), BF16),
        jax.ShapeDtypeStruct((OWNERS, PART, WIDE), BF16),
    ]
    product = lambda slots: pl.pallas_call(
        functools.partial(kernel, slots),
        out_shape=back,
        in_specs=[hbm] * 4,
        out_specs=[anywhere, anywhere],
        scratch_shapes=[
            pltpu.SMEM((4, 2, 4), jnp.int32),
            pltpu.SMEM((4, 2, 4), jnp.int32),
            vmem(SHOTS, MAIN, dtype=jnp.int32),
            pltpu.SMEM((SHOTS, MAIN), jnp.int32),
            vmem(2 * F, samples),
            vmem(SHOTS, SHARE // PART, PART, samples),
            vmem(SHOTS, receivers // PART, PART, samples),
            vmem(SHOTS * HALF, samples),
            vmem(OWNERS, slots, PART, MAIN),
            message(MAIN),
            message(tail_lanes(slots)),
            vmem(OWNERS, slots, PART, MAIN),
            message(MAIN),
            message(MAIN),
            message(tail_lanes(slots)),
            vmem(2, OWNERS * PART, MAIN, dtype=F32),
            vmem(BINS, WIDE, 2 * WIDE),
            vmem(POINTS * PART, MAIN, dtype=F32),
            vmem(2, POINTS * PART, MAIN, dtype=F32),
            vmem(OWNERS * SHOTS * PART, MAIN, dtype=F32),
            vmem(2, OWNERS * PART, MAIN, dtype=F32),
            vmem(OWNERS, SHOTS, PART, MAIN),
            message(WIDE),
            pltpu.SemaphoreType.DMA((9,)),
            pltpu.SemaphoreType.DMA((2,)),
            pltpu.SemaphoreType.DMA((5,)),
            pltpu.SemaphoreType.DMA((5,)),
        ],
        compiler_params=pltpu.CompilerParams(
            collective_id=slots // 2, has_side_effects=True, vmem_limit_bytes=50 * 2**20
        ),
    )
    points, gathers = surface_point.transpose(0, 2, 1), gather_index.transpose(0, 2, 1)
    blocks = traces.reshape(shots, receivers // PART, PART, samples)
    case = pl.pallas_call(
        choose,
        out_shape=jax.ShapeDtypeStruct((1,), jnp.int32),
        in_specs=[pl.BlockSpec(memory_space=pltpu.SMEM)],
        out_specs=pl.BlockSpec(memory_space=pltpu.SMEM),
    )(gathers)[0]
    spectra = lax.switch(case, [product(room) for room in ROOMS], points, gathers, blocks, jnp.asarray(table))
    return pl.pallas_call(
        inverse,
        out_shape=jax.ShapeDtypeStruct((shots, SHARE, samples), BF16),
        in_specs=[pl.BlockSpec(memory_space=pltpu.VMEM)] * 3,
        out_specs=anywhere,
        scratch_shapes=[
            vmem(SHOTS, SHARE, samples),
            pltpu.SemaphoreType.DMA((SHOTS // 2,)),
        ],
        compiler_params=pltpu.CompilerParams(vmem_limit_bytes=50 * 2**20),
    )(*spectra, jnp.asarray(table[:, : samples // 2]))


def solution(mesh):
    placed = (P("shot", None, None), P(), P())
    return jax.shard_map(
        shards, mesh=mesh, in_specs=placed, out_specs=P("shot", "surf", None), check_vma=False
    )
```

profile of v0, /device:TPU:1, one launch (start us, length us, event | category | flops | bytes accessed | tf_op | source)
XLA Modules:
  0.0 39.8 jit_solution(16094766052092757800)
XLA Ops:
  0.0 1.5 %shard_map.55 = s32[1]{0:T(128)} custom-call(s32[4,2,4]{2,1,0:T(2,128)} %bitcast.7), custom_call_target="tpu_custom_call" | custom-call | tf_op jit(solution)/shard_map/pallas_call | solution.py:345
  2.1 0.0 copy-start
  2.1 35.4 %conditional.1 = ((bf16[32,8,16,128]{3,2,1,0:T(8,128)(2,1)S(1)}, bf16[32,16,256]{2,1,0:T(8,128)(2,1)S(1)})) conditional(s32[]{:T(128)} %bitcast.1, (s32[4,2,4]{2,1,0:T(2,128)}, s32[4,2,4]{2,1,0:T(2,128)}, bf16[8,40,16,1024]{3,2,1,0:T(8,128)(2,1)}, bf16[512,1024]{1,0:T(8,128)(2,1)}) %tuple.27, (s32[4,2,4]{2,1,0:T(2,128)}, ...), branch_computations={%region_0.0_spmd, %region_1.0_spmd, %region_2.0_spmd} | conditional | bytes 8 | solution.py:351
  2.1 35.2 %branch_0_fun.1 = (bf16[32,8,16,128]{3,2,1,0:T(8,128)(2,1)S(1)}, bf16[32,16,256]{2,1,0:T(8,128)(2,1)S(1)}) custom-call(s32[4,2,4]{2,1,0:T(2,128)} %get-tuple-element.29.point_ref, s32[4,2,4]{2,1,0:T(2,128)} %get-tuple-element.30.gather_ref, bf16[8,40,16,1024]{3,2,1,0:T(8,128)(2,1)} %get-tuple-element.31.traces, bf16[512,1024]{1,0:T(8,128)(2,1)} %get-tuple-element.32.table), custom_call_target="tpu_custom_call" | custom-call | tf_op jit(solution)/shard_map/cond/branch_0_fun/pallas_call | solution.py:351
  37.6 0.0 copy-done
  37.6 2.0 %shard_map.56 = bf16[8,160,1024]{2,1,0:T(8,128)(2,1)} custom-call(bf16[32,8,16,128]{3,2,1,0:T(8,128)(2,1)S(1)} %get-tuple-element.43.hm, bf16[32,16,256]{2,1,0:T(8,128)(2,1)S(1)} %get-tuple-element.44.ht, bf16[512,512]{1,0:T(8,128)(2,1)S(1)} %copy-done), custom_call_target="tpu_custom_call" | custom-call | tf_op jit(solution)/shard_map/pallas_call | solution.py:352
Async XLA Ops:
  2.1 35.5 %copy-start = (bf16[512,512]{1,0:T(8,128)(2,1)S(1)}, bf16[512,512]{1,0:T(8,128)(2,1)}, u32[]{:S(2)}) copy-start(bf16[512,512]{1,0:T(8,128)(2,1)} %constant.11.clone.tab) | copy-start | bytes 1572868
where the time goes:
time: 40.5 us; the launch traced here: 39.8 us
  Pallas kernels  38.6 us (95%)
  between operations  0.88 us (2%)
    pallas_call x1, Pallas kernels, shards(): lax.switch(case, [product(room) for room in ROOMS], points, gathers, bloc...  35.2 us
    pallas_call x1, Pallas kernels, shards(): pl.pallas_call(inverse, out_shape=jax.ShapeDtypeStruct((shots, SHARE, sam...  1.99 us
    pallas_call x1, Pallas kernels, shards(): pl.pallas_call(choose, out_shape=jax.ShapeDtypeStruct((1,), jnp.int32), i...  1.46 us

commit v1 on v0

--- a/solution.py
+++ b/solution.py
@@ -94,10 +94,10 @@
     for load in loads[2:5]:
         load.start()
 
-    def start(way):
+    def start(way, order=everyone):
         kind, source, target = way
         pltpu.make_async_copy(source(me), target(me), recv_sem.at[kind]).start()
-        for n in everyone:
+        for n in order:
             pltpu.make_async_remote_copy(
                 src_ref=source(peers[n]),
                 dst_ref=target(me),
@@ -245,7 +245,7 @@
     for k in range(2):
         bm[:, 4 * k : 4 * k + 4] = totals[:, 4 * k : 4 * k + 4].astype(BF16)
         back_main = 4, four(bm, k), four(hm, k)
-        start(back_main)
+        start(back_main, everyone[16 * k :] + everyone[: 16 * k])
     arrive(3, ht)
     arrive(4, hm)
     for kind, whole in enumerate((st, sn, sm, bt, bm)):

time: 40.5 us -> 41 us (1.012)
  Pallas kernels: 38.6 us -> 39.1 us
    pallas_call x1, Pallas kernels: 35.2 us -> 35.6 us  [shards(): lax.switch(case, [product(room) for room in ROOMS], points, gathers, bloc...]
where the time goes in v1:
time: 41 us; the launch traced here: 40.3 us
  Pallas kernels  39.1 us (95%)
  between operations  0.88 us (2%)
    pallas_call x1, Pallas kernels, shards(): lax.switch(case, [product(room) for room in ROOMS], points, gathers, bloc...  35.6 us
    pallas_call x1, Pallas kernels, shards(): pl.pallas_call(inverse, out_shape=jax.ShapeDtypeStruct((shots, SHARE, sam...  1.99 us
    pallas_call x1, Pallas kernels, shards(): pl.pallas_call(choose, out_shape=jax.ShapeDtypeStruct((1,), jnp.int32), i...  1.46 us

profile of v1, /device:TPU:1, one launch (start us, length us, event | category | flops | bytes accessed | tf_op | source)
XLA Modules:
  0.0 40.3 jit_solution(12329551147420138191)
XLA Ops:
  0.0 1.5 %shard_map.55 = s32[1]{0:T(128)} custom-call(s32[4,2,4]{2,1,0:T(2,128)} %bitcast.7), custom_call_target="tpu_custom_call" | custom-call | tf_op jit(solution)/shard_map/pallas_call | solution.py:345
  2.1 0.0 copy-start
  2.1 35.9 %conditional.1 = ((bf16[32,8,16,128]{3,2,1,0:T(8,128)(2,1)S(1)}, bf16[32,16,256]{2,1,0:T(8,128)(2,1)S(1)})) conditional(s32[]{:T(128)} %bitcast.1, (s32[4,2,4]{2,1,0:T(2,128)}, s32[4,2,4]{2,1,0:T(2,128)}, bf16[8,40,16,1024]{3,2,1,0:T(8,128)(2,1)}, bf16[512,1024]{1,0:T(8,128)(2,1)}) %tuple.27, (s32[4,2,4]{2,1,0:T(2,128)}, ...), branch_computations={%region_0.0_spmd, %region_1.0_spmd, %region_2.0_spmd} | conditional | bytes 8 | solution.py:351
  2.1 35.6 %branch_0_fun.1 = (bf16[32,8,16,128]{3,2,1,0:T(8,128)(2,1)S(1)}, bf16[32,16,256]{2,1,0:T(8,128)(2,1)S(1)}) custom-call(s32[4,2,4]{2,1,0:T(2,128)} %get-tuple-element.29.point_ref, s32[4,2,4]{2,1,0:T(2,128)} %get-tuple-element.30.gather_ref, bf16[8,40,16,1024]{3,2,1,0:T(8,128)(2,1)} %get-tuple-element.31.traces, bf16[512,1024]{1,0:T(8,128)(2,1)} %get-tuple-element.32.table), custom_call_target="tpu_custom_call" | custom-call | tf_op jit(solution)/shard_map/cond/branch_0_fun/pallas_call | solution.py:351
  38.1 0.0 copy-done
  38.1 2.0 %shard_map.56 = bf16[8,160,1024]{2,1,0:T(8,128)(2,1)} custom-call(bf16[32,8,16,128]{3,2,1,0:T(8,128)(2,1)S(1)} %get-tuple-element.43.hm, bf16[32,16,256]{2,1,0:T(8,128)(2,1)S(1)} %get-tuple-element.44.ht, bf16[512,512]{1,0:T(8,128)(2,1)S(1)} %copy-done), custom_call_target="tpu_custom_call" | custom-call | tf_op jit(solution)/shard_map/pallas_call | solution.py:352
Async XLA Ops:
  2.1 36.0 %copy-start = (bf16[512,512]{1,0:T(8,128)(2,1)S(1)}, bf16[512,512]{1,0:T(8,128)(2,1)}, u32[]{:S(2)}) copy-start(bf16[512,512]{1,0:T(8,128)(2,1)} %constant.11.clone.tab) | copy-start | bytes 1572868
